TPU v7x, 512 devices: a whole 4x4x16 slice. The times are simulated.
512 devices in a mesh: prow: 32 (over z, core), pcol: 16 (over y, x).
Axes of the slice: x: 4, y: 4, z: 16, core: 2. Of those that a mesh axis runs over, the one named last changes fastest.
Arguments:
- diag_block: float32 [256, 256], P('prow'), as said below
- panel: float32 [65536, 256], P(('prow', 'pcol')), may hold values from -4 to 4
- trailing: float32 [65536, 4096], P('prow', 'pcol'), may hold values from -6 to 6
Outputs:
- updated: float32 [65536, 4096], P('prow', 'pcol')
- solved: float32 [65536, 256], P(('prow', 'pcol'))
Inputs may be any that keep to these rules, and one draw needn't show every extreme that they name: diag_block is symmetric positive definite.
All inputs are finite; a program needn't handle non-finite values.
Results may differ from a plain program's by a relative error of at most 0.00007.
Values sent between devices are 32-bit elements; how exact they have to be, the bound alone decides.
A program may use at most 64 MiB of HBM per device.

v0:
```python
import jax
import jax.numpy as jnp
from jax import lax
from jax.sharding import PartitionSpec as P


def per_device(diag_block, panel, trailing):
    whole_diag = lax.all_gather(diag_block, "prow", axis=0, tiled=True)
    width = whole_diag.shape[0]
    factor = jnp.linalg.cholesky(whole_diag)
    identity = jnp.eye(width, dtype=jnp.float32)
    inverse = lax.linalg.triangular_solve(factor, identity, left_side=True, lower=True)
    own_solved = jnp.dot(
        panel, inverse.T, precision=lax.Precision.HIGHEST, preferred_element_type=jnp.float32
    )
    row_panel = lax.all_gather(own_solved, "pcol", axis=0, tiled=True)
    lead_tile = row_panel[:width]
    every_tile = lax.all_gather(lead_tile, "prow", axis=0, tiled=True)
    partner = lax.dynamic_slice_in_dim(every_tile, lax.axis_index("pcol") * width, width, 0)
    product = lax.dot_general(
        row_panel,
        partner,
        (((1,), (1,)), ((), ())),
        precision=lax.Precision.HIGHEST,
        preferred_element_type=jnp.float32,
    )
    updated = trailing - product
    return (updated, own_solved)


def solution(mesh):
    in_specs = (P("prow", None), P(("prow", "pcol"), None), P("prow", "pcol"))
    out_specs = (P("prow", "pcol"), P(("prow", "pcol"), None))
    return jax.shard_map(
        per_device, mesh=mesh, in_specs=in_specs, out_specs=out_specs, check_vma=False
    )
```

profile of v0, /device:TPU:1, one launch (start us, length us, event | category | flops | bytes accessed | tf_op | source)
XLA Modules:
  0.0 261.7 jit_solution(7643315962689769503)
XLA Ops:
  7.2 0.0 copy-start
  7.2 0.0 all-gather.3.cloned.1.call-start
  7.3 38.5 %all_gather.9 = f32[256,256]{1,0:T(8,128)S(1)} all-gather(f32[8,256]{1,0:T(8,128)} %param.3), channel_id=1, replica_groups=mesh['prow'=32,'pcol'=16] {'prow'}, dimensions={0}, use_global_device_ids=true | all-gather | bytes 270336 | tf_op jit(solution)/shard_map/all_gather | solution.py:8
  45.8 0.1 copy.8
  46.0 11.7 %cholesky.50 = f32[128,128]{1,0:T(8,128)S(1)} custom-call(f32[128,128]{1,0:T(8,128)S(1)} %cholesky.118), custom_call_target="Cholesky" | custom-call | tf_op jit(solution)/shard_map/jit(cholesky)/cholesky | solution.py:10
  57.8 9.8 %custom-call.14 = f32[1,128,128]{1,2,0:T(8,128)S(1)} custom-call(f32[1,128,128]{2,1,0:T(8,128)S(1)} %get-tuple-element.27), custom_call_target="InvertDiagBlocksLowerTriangular" | custom-call | tf_op jit(solution)/shard_map/jit(cholesky)/cholesky | solution.py:10
  67.6 0.2 constant_dynamic-update-slice_fusion
  67.8 0.3 convolution_subtract_fusion.2
  68.1 0.0 copy-start.1
  68.1 11.7 %cholesky.105 = f32[128,128]{1,0:T(8,128)S(1)} custom-call(f32[128,128]{1,0:T(8,128)S(1)} %convolution_subtract_fusion.2), custom_call_target="Cholesky" | custom-call | tf_op jit(solution)/shard_map/jit(cholesky)/cholesky | solution.py:10
  79.8 0.7 compare_reduce_fusion
  81.9 0.1 triangular_solve.63
  81.9 4.1 %while.1 = (s32[]{:T(128)}, f32[256,256]{1,0:T(8,128)S(1)}, s32[2,2]{1,0:T(2,128)S(1)}, f32[2,128,128]{2,1,0:T(8,128)S(1)}, s32[]{:T(128)}) while((s32[]{:T(128)}, f32[256,256]{1,0:T(8,128)S(1)}, s32[2,2]{1,0:T(2,128)S(1)}, f32[2,128,128]{2,1,0:T(8,128)S(1)}, s32[]{:T(128)}) %tuple.29), condition=%wide.while_cond, body=%wide.while_body.sunk | while | flops 2 | bytes 131189 | solution.py:12
  82.1 0.6 fusion.22
  82.7 1.4 bitcast_dynamic-update-slice_fusion.2
  84.1 0.6 fusion.22
  84.7 1.4 bitcast_dynamic-update-slice_fusion.2
  86.0 19.7 %custom-call.15 = f32[2,128,128]{1,2,0:T(8,128)S(1)} custom-call(f32[2,128,128]{2,1,0:T(8,128)S(1)} %get-tuple-element.9), custom_call_target="InvertDiagBlocksLowerTriangular" | custom-call | tf_op jit(solution)/shard_map/triangular_solve | solution.py:12
  105.7 0.3 fusion.5
  106.0 0.3 convolution_subtract_fusion.1
  106.3 0.3 fusion.8
  106.6 0.0 copy-done
  106.6 1.0 convolution_bitcast_fusion
  107.7 0.0 all-gather.3.cloned.1.call-update
  107.7 0.0 all-gather.5.cloned.1.call-start
  107.7 57.7 %all-gather.3.cloned.1.call-done = f32[2048,256]{0,1:T(8,128)} async-done(((f32[128,256]{0,1:T(8,128)}), f32[2048,256]{0,1:T(8,128)}) %all-gather.3.cloned.1.call-update) | async-done | bytes 2097168 | tf_op jit(solution)/shard_map/all_gather | solution.py:16
  165.4 1.7 slice.58
  167.1 0.0 all-gather.5.cloned.1.call-update
  167.1 1.7 copy.9
  168.8 79.8 %all-gather.5.cloned.1.call-done = f32[8192,256]{0,1:T(8,128)} async-done(((f32[256,256]{0,1:T(8,128)}), f32[8192,256]{0,1:T(8,128)}) %all-gather.5.cloned.1.call-update) | async-done | bytes 8388624 | tf_op jit(solution)/shard_map/all_gather | solution.py:18
  248.5 0.0 copy-done.1
  248.6 6.4 %convolution_subtract_fusion = f32[2048,256]{1,0:T(8,128)} fusion(f32[2048,256]{1,0:T(8,128)S(1)} %copy-done.1, f32[2048,256]{0,1:T(8,128)} %all-gather.3.cloned.1.call-done, f32[8192,256]{0,1:T(8,128)} %all-gather.5.cloned.1.call-done, s32[]{:T(128)S(6)} %select_n.8), kind=kOutput, calls=%fused_computation.2 | convolution fusion | flops 1611137024 | bytes 6553604 | tf_op jit(solution)/shard_map/dot_general | solution.py:20
  (11 shorter events, 0.2 us)
Async XLA Ops:
  7.2 99.4 %copy-start = (f32[128,256]{1,0:T(8,128)S(1)}, f32[128,256]{1,0:T(8,128)}, u32[]{:S(2)}) copy-start(f32[128,256]{1,0:T(8,128)} %param.4) | copy-start | bytes 393220
  7.2 158.3 %all-gather.3.cloned.1.call-start = ((), (), s32[]{:S(2)}) async-start(), calls=%async_computation | async-start | bytes 2228224 | tf_op jit(solution)/shard_map/all_gather | solution.py:16
  68.1 180.5 %copy-start.1 = (f32[2048,256]{1,0:T(8,128)S(1)}, f32[2048,256]{1,0:T(8,128)}, u32[]{:S(2)}) copy-start(f32[2048,256]{1,0:T(8,128)} %param.5) | copy-start | bytes 6291460
  107.7 140.9 %all-gather.5.cloned.1.call-start = ((), (), s32[]{:S(2)}) async-start(), calls=%async_computation.1 | async-start | bytes 8650752 | tf_op jit(solution)/shard_map/all_gather | solution.py:18
Sparse Core Ops, SparseCore 0:
  107.8 57.5 all-gather.2
  168.2 80.3 all-gather.4
where the time goes:
time: 262 us
  waiting for transfers between devices  137 us (52%)
  other arithmetic  53.8 us (21%)
  blocking collectives  38.5 us (15%)
  between operations  15.5 us (6%)
  matrix products  8.71 us (3%)
  local copies, waits for them, and re-layouts  7.49 us (3%)
    all_gather x1, waiting for transfers between devices, per_device(): every_tile = lax.all_gather(lead_tile, 'prow', axis=0, tiled=True)  79.8 us
    all_gather x1, waiting for transfers between devices, per_device(): row_panel = lax.all_gather(own_solved, 'pcol', axis=0, tiled=True)  57.7 us
    all_gather x1, blocking collectives, per_device(): whole_diag = lax.all_gather(diag_block, 'prow', axis=0, tiled=True)  38.5 us
    another operation x6, other arithmetic, per_device(): factor = jnp.linalg.cholesky(whole_diag)  34 us
    another operation x3, other arithmetic, per_device(): lax.linalg.triangular_solve(factor, identity, left_side=True, lower=True)  19.7 us
    dot_general x1, matrix products, per_device(): lax.dot_general(row_panel, partner, (((1,), (1,)), ((), ())), precision=l...  6.36 us
  transfers between devices with their start and end apart: 2, of which 2 were waited for; matrix products, arithmetic and copies ran while one was open for 1% of the time, Pallas kernels for 0%

commit v1 on v0

v1 whole, which is shorter than its diff:
```python
import functools

import jax
import jax.numpy as jnp
from jax import lax
from jax.experimental import pallas as pl
from jax.experimental.pallas import tpu as pltpu
from jax.sharding import PartitionSpec as P

HI = lax.Precision.HIGHEST
F32 = jnp.float32
NBK = 16
H = 128

def sub(x, s):
    return jnp.broadcast_to(x[s:s + 1, :], (8, 128))

def lane(x, c):
    return jnp.broadcast_to(x[:, c:c + 1], (8, 128))

def dot_tn(a, b):
    return lax.dot_general(a, b, (((0,), (0,)), ((), ())), precision=HI, preferred_element_type=F32)

def dot_nn(a, b):
    return lax.dot_general(a, b, (((1,), (0,)), ((), ())), precision=HI, preferred_element_type=F32)

def dot_nt(a, b):
    return lax.dot_general(a, b, (((1,), (1,)), ((), ())), precision=HI, preferred_element_type=F32)


def stage(e_ref, r_ref, u_ref, y_ref, tiles, unroll=False):
    iota = lax.broadcasted_iota(jnp.int32, (8, 128), 0)

    def body(k, carry):
        u_prev = u_ref[...]
        e_ref[0:H, :] = e_ref[0:H, :] - dot_tn(u_prev[:, 0:H], u_prev)

        r = [[r_ref[8 * g:8 * g + 8, 128 * t:128 * t + 128] for t in range(tiles + 1)] for g in range(2)]
        b = [[lane(r[g][0], j) if (g == 1 or j < 8) else None for g in range(2)] for j in range(16)]
        rot = [pltpu.roll(r[g][0], H - NBK, 1) for g in range(2)]
        nxt = jnp.concatenate(rot, axis=0).T[0:16, :]
        gm = [[lane(nxt[8 * g:8 * g + 8, :], j) for g in range(2)] for j in range(16)]
        for g in range(2):
            r[g][0] = rot[g]
        scale = [None, None]
        rows = []
        gs = []
        for j in range(16):
            gj, sj = divmod(j, 8)
            p = sub(b[j][gj], sj)
            f = 1.0 / p
            rs = lax.rsqrt(p)
            m = [None, None]
            for g in range(gj, 2):
                m[g] = b[j][g] * f
            scale[gj] = rs if sj == 0 else jnp.where(iota >= sj, rs, scale[gj])
            g0 = gm[j][0] * f
            g1 = gm[j][1] * f
            gs.append((g0, g1))
            for c in range(j + 1, 16):
                gc, sc = divmod(c, 8)
                a = sub(b[j][gc], sc)
                for g in range(gc, 2):
                    b[c][g] = b[c][g] - m[g] * a
                gm[c][0] = gm[c][0] - g0 * a
                gm[c][1] = gm[c][1] - g1 * a
            row = [sub(r[gj][t], sj) for t in range(tiles + 1)]
            rows.append(row)
            for g in range(gj, 2):
                mm = jnp.where(iota > sj, m[g], 0.0) if g == gj else m[g]
                if g == gj and sj == 7:
                    continue
                for t in range(tiles + 1):
                    r[g][t] = r[g][t] - mm * row[t]
        base = pl.multiple_of((k + 1) * NBK, NBK)
        for g in range(2):
            for t in range(tiles + 1):
                acc = e_ref[pl.ds(base + 8 * g, 8), 128 * t:128 * t + 128]
                if t == 0:
                    acc = pltpu.roll(acc, lax.rem(2 * H - NBK * (k + 1), H), 1)
                for j in range(16):
                    acc = acc - gs[j][g] * rows[j][t]
                r_ref[8 * g:8 * g + 8, 128 * t:128 * t + 128] = acc
        here = pl.multiple_of(k * NBK, NBK)
        for g in range(2):
            for t in range(tiles + 1):
                v = r[g][t] * scale[g]
                if t == 0:
                    v = pltpu.roll(v, lax.rem(NBK * (k + 1), H), 1)
                else:
                    y_ref[pl.ds(here + 8 * g, 8), 128 * (t - 1):128 * t] = v
                u_ref[8 * g:8 * g + 8, 128 * t:128 * t + 128] = v
        return carry

    r_ref[...] = e_ref[0:16, :]
    u_ref[...] = jnp.zeros_like(u_ref)
    if unroll:
        for k in range(8):
            body(k, 0)
    else:
        lax.fori_loop(0, 8, body, 0)


def chol_inverse(a_ref, w_ref, e1, r1, u1, y1, e2, r2, u2, y2, unroll=False):
    eye = (lax.broadcasted_iota(jnp.int32, (H, H), 0) == lax.broadcasted_iota(jnp.int32, (H, H), 1)).astype(F32)
    e1[0:H, 0:2 * H] = a_ref[0:H, :]
    e1[0:H, 2 * H:3 * H] = eye
    e1[H:, :] = jnp.zeros_like(e1[H:, :])
    stage(e1, r1, u1, y1, 2, unroll)
    u12 = y1[:, 0:H]
    e2[0:H, 0:H] = a_ref[H:2 * H, H:2 * H] - dot_tn(u12, u12)
    e2[0:H, H:2 * H] = eye
    e2[H:, :] = jnp.zeros_like(e2[H:, :])
    v = dot_tn(u12, y1[:, H:2 * H])
    stage(e2, r2, u2, y2, 1, unroll)
    w_ref[0:H, 0:H] = y1[:, H:2 * H]
    w_ref[0:H, H:2 * H] = jnp.zeros((H, H), F32)
    w_ref[H:2 * H, 0:H] = -dot_nn(y2[...], v)
    w_ref[H:2 * H, H:2 * H] = y2[...]


SCRATCH = [pltpu.VMEM((144, 384), F32), pltpu.VMEM((16, 384), F32), pltpu.VMEM((16, 384), F32), pltpu.VMEM((128, 256), F32),
           pltpu.VMEM((144, 256), F32), pltpu.VMEM((16, 256), F32), pltpu.VMEM((16, 256), F32), pltpu.VMEM((128, 128), F32)]


MESH = pl.DeviceIdType.MESH
BF16 = jnp.bfloat16


def remote(src, dst, send, recv, to):
    return pltpu.make_async_remote_copy(
        src_ref=src, dst_ref=dst, send_sem=send, recv_sem=recv, device_id=to, device_id_type=MESH
    )


def gather_and_factor(
    diag_ref, panel_ref, pa_ref, pb_ref, q_ref, w_ref,
    d_ref, a_ref, e1, r1, u1, y1, e2, r2, u2, y2,
    d1_send, d1_recv, d2_send, d2_recv, q1_send, q1_recv, q2_send, q2_recv, q3_send, q3_recv,
    xa_send, xa_recv, yb_send, yb_recv, ya_send, ya_recv, xb_send, xb_recv, own_sem,
):
    prow, pcol = lax.axis_index("prow"), lax.axis_index("pcol")
    z, core = prow // 2, prow % 2
    y, x = pcol // 4, pcol % 4
    peer = (z * 2 + 1 - core, pcol)
    source = jnp.logical_and(prow < 16, pcol < 2)
    self_lead = jnp.logical_and(source, prow == pcol)

    def along_z(d):
        return (lax.rem(z + d, 16) * 2 + core, pcol)

    def along_x(d):
        return (prow, y * 4 + lax.rem(x + d, 4))

    def along_y(d):
        return (prow, lax.rem(y + d, 4) * 4 + x)

    barrier = pltpu.get_barrier_semaphore()

    def greet(to):
        pl.semaphore_signal(barrier, inc=1, device_id=to, device_id_type=MESH)

    def greet_z(d, carry):
        greet(along_z(d))
        return carry

    greet(peer)
    for d in (1, 2, 3):
        greet(along_x(d))
        greet(along_y(d))

    @pl.when(jnp.logical_not(self_lead))
    def _():
        greet((pcol, core))

    lax.fori_loop(1, 16, greet_z, 0)
    extra = jnp.where(source, 16, 0) - jnp.where(self_lead, 1, 0)
    pl.semaphore_wait(barrier, 22 + extra)

    def d1(d):
        return remote(diag_ref, d_ref.at[core, z], d1_send.at[d], d1_recv.at[d], along_z(d))

    def start_d1(d, carry):
        d1(d).start()
        return carry

    lax.fori_loop(1, 16, start_d1, 0)

    def q1(t):
        rows = panel_ref.at[pl.ds(pl.multiple_of(t * 8, 8), 8), :]
        return remote(rows, q_ref.at[pcol, t], q1_send.at[t], q1_recv.at[0], (t * 2 + pcol, prow))

    own_lead = pltpu.make_async_copy(panel_ref.at[pl.ds(0, 8), :], q_ref.at[core, z], own_sem.at[2])

    @pl.when(source)
    def _():
        def start_q1(t, carry):
            @pl.when(jnp.logical_not(jnp.logical_and(self_lead, t == 0)))
            def _():
                q1(t).start()
            return carry

        lax.fori_loop(0, 16, start_q1, 0)

    @pl.when(self_lead)
    def _():
        own_lead.start()

    top, low = panel_ref.at[pl.ds(0, 64), :], panel_ref.at[pl.ds(64, 64), :]

    def xa(d):
        return remote(top, pa_ref.at[y, x], xa_send.at[d], xa_recv.at[d], along_x(d))

    def yb(d):
        return remote(low, pb_ref.at[y, x], yb_send.at[d], yb_recv.at[d], along_y(d))

    own_top = pltpu.make_async_copy(top, pa_ref.at[y, x], own_sem.at[0])
    own_low = pltpu.make_async_copy(low, pb_ref.at[y, x], own_sem.at[1])
    for d in (1, 3, 2):
        xa(d).start()
        yb(d).start()
    own_top.start()
    own_low.start()
    d_ref[core, z] = diag_ref[...]

    def wait_d1(d, carry):
        d1(d).wait()
        return carry

    lax.fori_loop(1, 16, wait_d1, 0)
    d2 = remote(d_ref.at[core], d_ref.at[core], d2_send.at[0], d2_recv.at[0], peer)
    d2.start()

    @pl.when(jnp.logical_not(self_lead))
    def _():
        remote(q_ref.at[core, z], q_ref.at[core, z], q1_send.at[0], q1_recv.at[0], peer).wait_recv()

    @pl.when(self_lead)
    def _():
        own_lead.wait()

    def q2(d):
        return remote(q_ref.at[core, z], q_ref.at[core, z], q2_send.at[d], q2_recv.at[d], along_z(d))

    def start_q2(d, carry):
        q2(d).start()
        return carry

    lax.fori_loop(1, 16, start_q2, 0)

    own_top.wait()
    own_low.wait()
    for d in (1, 3, 2):
        xa(d).wait()
        yb(d).wait()

    def ya(d):
        return remote(pa_ref.at[y], pa_ref.at[y], ya_send.at[d], ya_recv.at[d], along_y(d))

    def xb(d):
        return remote(pb_ref.at[:, x], pb_ref.at[:, x], xb_send.at[d], xb_recv.at[d], along_x(d))

    for d in (1, 3, 2):
        ya(d).start()
        xb(d).start()

    d2.wait()
    for t in range(16):
        for c in range(2):
            a_ref[t * 16 + c * 8:t * 16 + c * 8 + 8, :] = d_ref[c, t]

    chol_inverse(a_ref, w_ref, e1, r1, u1, y1, e2, r2, u2, y2)

    def wait_q2(d, carry):
        q2(d).wait()
        return carry

    lax.fori_loop(1, 16, wait_q2, 0)
    q3 = remote(q_ref.at[core], q_ref.at[core], q3_send.at[0], q3_recv.at[0], peer)
    q3.start()

    @pl.when(source)
    def _():
        def wait_q1(t, carry):
            @pl.when(jnp.logical_not(jnp.logical_and(self_lead, t == 0)))
            def _():
                q1(t).wait_send()
            return carry

        lax.fori_loop(0, 16, wait_q1, 0)

    for d in (1, 3, 2):
        ya(d).wait()
        xb(d).wait()
    q3.wait()


def halves(v):
    high = v.astype(BF16)
    return high, (v - high.astype(F32)).astype(BF16)


def dot3(a, b):
    def one(p, q):
        return lax.dot_general(p, q, (((1,), (1,)), ((), ())), preferred_element_type=F32)

    return one(a[0], b[0]) + (one(a[0], b[1]) + one(a[1], b[0]))


def update(pa_ref, pb_ref, t_ref, w_ref, q_ref, own_ref, u_ref, s_ref, wh, wl, qh, ql):
    @pl.when(pl.program_id(0) == 0)
    def _():
        w = halves(w_ref[...])
        wh[...], wl[...] = w
        qh[...], ql[...] = halves(dot3(halves(q_ref[...]), w))
        s_ref[...] = dot3(halves(own_ref[...]), w)

    rows = jnp.concatenate([pa_ref[0], pb_ref[0], pa_ref[1], pb_ref[1]], axis=0)
    solved = dot3(halves(rows), (wh[...], wl[...]))
    u_ref[...] = t_ref[...] - dot3(halves(solved), (qh[...], ql[...]))


def per_device(diag_block, panel, trailing):
    hbm = pl.BlockSpec(memory_space=pl.ANY)
    vmem = pl.BlockSpec(memory_space=pltpu.VMEM)
    dma = pltpu.SemaphoreType.DMA
    pa, pb, q, w = pl.pallas_call(
        gather_and_factor,
        out_shape=(
            jax.ShapeDtypeStruct((4, 4, 64, 256), F32),
            jax.ShapeDtypeStruct((4, 4, 64, 256), F32),
            jax.ShapeDtypeStruct((2, 16, 8, 256), F32),
            jax.ShapeDtypeStruct((256, 256), F32),
        ),
        in_specs=[vmem, hbm],
        out_specs=(hbm, hbm, hbm, vmem),
        scratch_shapes=[pltpu.VMEM((2, 16, 8, 256), F32), pltpu.VMEM((256, 256), F32)] + SCRATCH + [
            dma((16,)), dma((16,)), dma((1,)), dma((1,)), dma((16,)), dma((1,)), dma((16,)), dma((16,)), dma((1,)), dma((1,)),
            dma((4,)), dma((4,)), dma((4,)), dma((4,)), dma((4,)), dma((4,)), dma((4,)), dma((4,)), dma((3,)),
        ],
        compiler_params=pltpu.CompilerParams(collective_id=0, has_side_effects=True, vmem_limit_bytes=32 << 20),
    )(diag_block, panel)
    pa, pb, q = pa.reshape(16, 64, 256), pb.reshape(16, 64, 256), q.reshape(256, 256)

    def whole(rows):
        return pl.BlockSpec((rows, 256), lambda i: (0, 0))

    return pl.pallas_call(
        update,
        grid=(8,),
        out_shape=(jax.ShapeDtypeStruct((2048, 256), F32), jax.ShapeDtypeStruct((128, 256), F32)),
        in_specs=[
            pl.BlockSpec((2, 64, 256), lambda i: (i, 0, 0)),
            pl.BlockSpec((2, 64, 256), lambda i: (i, 0, 0)),
            pl.BlockSpec((256, 256), lambda i: (i, 0)),
            whole(256), whole(256), whole(128),
        ],
        out_specs=(pl.BlockSpec((256, 256), lambda i: (i, 0)), whole(128)),
        scratch_shapes=[pltpu.VMEM((256, 256), BF16)] * 4,
        compiler_params=pltpu.CompilerParams(vmem_limit_bytes=32 << 20),
    )(pa, pb, trailing, w, q, panel)


def solution(mesh):
    in_specs = (P("prow", None), P(("prow", "pcol"), None), P("prow", "pcol"))
    out_specs = (P("prow", "pcol"), P(("prow", "pcol"), None))
    return jax.shard_map(
        per_device, mesh=mesh, in_specs=in_specs, out_specs=out_specs, check_vma=False
    )
```

time: 262 us -> 55.8 us (0.21)
  the two profiles are of different devices: /device:TPU:1 before, /device:TPU:13 now
where the time goes in v1:
time: 55.8 us; the launch traced here: 55.6 us
  Pallas kernels  51.7 us (93%)
  local copies, waits for them, and re-layouts  3.18 us (6%)
  between operations  0.66 us (1%)
    pallas_call x1, Pallas kernels, per_device(): pl.pallas_call(gather_and_factor, out_shape=(jax.ShapeDtypeStruct((4, 4,...  45.3 us
    pallas_call x1, Pallas kernels, per_device(): pl.pallas_call(update, grid=(8,), out_shape=(jax.ShapeDtypeStruct((2048,...  6.48 us
    unnamed x6, local copies, waits for them, and re-layouts  3.18 us

profile of v1, /device:TPU:13, one launch (start us, length us, event | category | flops | bytes accessed | tf_op | source)
XLA Modules:
  0.0 55.6 jit_solution(17535937924683483007)
XLA Ops:
  0.6 0.0 copy-start.1
  0.6 0.9 %copy-done.1 = f32[128,256]{1,0:T(8,128)S(1)} copy-done((f32[128,256]{1,0:T(8,128)S(1)}, f32[128,256]{1,0:T(8,128)}, u32[]{:S(2)}) %copy-start.1) | copy-done | bytes 131096
  1.5 0.0 copy-start.2
  1.5 0.7 %copy-done.2 = f32[8,256]{1,0:T(8,128)S(1)} copy-done((f32[8,256]{1,0:T(8,128)S(1)}, f32[8,256]{1,0:T(8,128)}, u32[]{:S(2)}) %copy-start.2) | copy-done | bytes 8216
  2.2 45.3 %shard_map.50 = (f32[4,4,64,256]{3,2,1,0:T(8,128)S(1)}, f32[4,4,64,256]{3,2,1,0:T(8,128)S(1)}, f32[2,16,8,256]{3,2,1,0:T(8,128)S(1)}, f32[256,256]{1,0:T(8,128)S(1)}) custom-call(f32[8,256]{1,0:T(8,128)S(1)} %copy-done.2, f32[128,256]{1,0:T(8,128)S(1)} %copy-done.1), custom_call_target="tpu_custom_call" | custom-call | tf_op jit(solution)/shard_map/pallas_call | solution.py:327
  47.5 0.0 copy-start
  47.5 1.6 %copy-done = f32[2048,256]{1,0:T(8,128)S(1)} copy-done((f32[2048,256]{1,0:T(8,128)S(1)}, f32[2048,256]{1,0:T(8,128)}, u32[]{:S(2)}) %copy-start) | copy-done | bytes 2097176
  49.1 6.5 %shard_map.51 = (f32[2048,256]{1,0:T(8,128)}, f32[128,256]{1,0:T(8,128)}) custom-call(f32[16,64,256]{2,1,0:T(8,128)S(1)} %bitcast.3, f32[16,64,256]{2,1,0:T(8,128)S(1)} %bitcast.4, f32[2048,256]{1,0:T(8,128)S(1)} %copy-done, f32[256,256]{1,0:T(8,128)S(1)} %get-tuple-element.8.w_ref, f32[256,256]{1,0:T(8,128)S(1)} %bitcast.5, f32[128,256]{1,0:T(8,128)S(1)} %copy-done.1), custom_call_target="tpu_custom_call" | custom-call | tf_op jit(solution)/shard_map/pallas_call | solution.py:348
Async XLA Ops:
  0.6 0.9 %copy-start.1 = (f32[128,256]{1,0:T(8,128)S(1)}, f32[128,256]{1,0:T(8,128)}, u32[]{:S(2)}) copy-start(f32[128,256]{1,0:T(8,128)} %own_ref.1) | copy-start | bytes 393220
  1.5 0.7 %copy-start.2 = (f32[8,256]{1,0:T(8,128)S(1)}, f32[8,256]{1,0:T(8,128)}, u32[]{:S(2)}) copy-start(f32[8,256]{1,0:T(8,128)} %diag_ref.1) | copy-start | bytes 24580
  47.5 1.6 %copy-start = (f32[2048,256]{1,0:T(8,128)S(1)}, f32[2048,256]{1,0:T(8,128)}, u32[]{:S(2)}) copy-start(f32[2048,256]{1,0:T(8,128)} %t_ref.1) | copy-start | bytes 6291460

commit v2 on v1

--- a/solution.py
+++ b/solution.py
@@ -28,12 +28,23 @@
     return lax.dot_general(a, b, (((1,), (1,)), ((), ())), precision=HI, preferred_element_type=F32)
 
 
+def update_tn(u):
+    rest = u
+    parts = []
+    for _ in range(3):
+        parts.append(rest.astype(jnp.bfloat16))
+        rest = rest - parts[-1].astype(F32)
+    h, m, l = parts
+    left = jnp.concatenate([p[:, 0:H] for p in (h, h, h, m, m, l)], axis=0)
+    right = jnp.concatenate([h, m, l, h, m, h], axis=0)
+    return lax.dot_general(left, right, (((0,), (0,)), ((), ())), preferred_element_type=F32)
+
+
 def stage(e_ref, r_ref, u_ref, y_ref, tiles, unroll=False):
     iota = lax.broadcasted_iota(jnp.int32, (8, 128), 0)
 
     def body(k, carry):
-        u_prev = u_ref[...]
-        e_ref[0:H, :] = e_ref[0:H, :] - dot_tn(u_prev[:, 0:H], u_prev)
+        e_ref[0:H, :] = e_ref[0:H, :] - update_tn(u_ref[...])
 
         r = [[r_ref[8 * g:8 * g + 8, 128 * t:128 * t + 128] for t in range(tiles + 1)] for g in range(2)]
         b = [[lane(r[g][0], j) if (g == 1 or j < 8) else None for g in range(2)] for j in range(16)]
@@ -47,13 +58,18 @@
         gs = []
         for j in range(16):
             gj, sj = divmod(j, 8)
-            p = sub(b[j][gj], sj)
+            if j == 0:
+                p = sub(b[0][0], 0)
             f = 1.0 / p
             rs = lax.rsqrt(p)
             m = [None, None]
             for g in range(gj, 2):
                 m[g] = b[j][g] * f
             scale[gj] = rs if sj == 0 else jnp.where(iota >= sj, rs, scale[gj])
+            if j < 15:
+                gn, sn = divmod(j + 1, 8)
+                across = sub(b[j][gn], sn)
+                p = sub(b[j + 1][gn], sn) - (across * across) * f
             g0 = gm[j][0] * f
             g1 = gm[j][1] * f
             gs.append((g0, g1))
@@ -133,10 +149,21 @@
     )
 
 
+def each_along_z(act):
+    act(8)
+
+    def pair(k, carry):
+        act(8 - k)
+        act(8 + k)
+        return carry
+
+    lax.fori_loop(1, 8, pair, 0)
+
+
 def gather_and_factor(
     diag_ref, panel_ref, pa_ref, pb_ref, q_ref, w_ref,
-    d_ref, a_ref, e1, r1, u1, y1, e2, r2, u2, y2,
-    d1_send, d1_recv, d2_send, d2_recv, q1_send, q1_recv, q2_send, q2_recv, q3_send, q3_recv,
+    own_ref, d_ref, a_ref, e1, r1, u1, y1, e2, r2, u2, y2,
+    d1_send, d1_recv, dy_send, dy_recv, d2_send, d2_recv, q1_send, q1_recv, q2_send, q2_recv, q3_send, q3_recv,
     xa_send, xa_recv, yb_send, yb_recv, ya_send, ya_recv, xb_send, xb_recv, own_sem,
 ):
     prow, pcol = lax.axis_index("prow"), lax.axis_index("pcol")
@@ -160,77 +187,101 @@
     def greet(to):
         pl.semaphore_signal(barrier, inc=1, device_id=to, device_id_type=MESH)
 
-    def greet_z(d, carry):
-        greet(along_z(d))
-        return carry
-
-    greet(peer)
+    each_along_z(lambda d: greet(along_z(d)))
+
+    @pl.when(jnp.logical_not(self_lead))
+    def _():
+        greet((pcol, core))
+
     for d in (1, 2, 3):
         greet(along_x(d))
         greet(along_y(d))
-
-    @pl.when(jnp.logical_not(self_lead))
+    greet(peer)
+
+    own = [
+        pltpu.make_async_copy(panel_ref, own_ref, own_sem.at[0]),
+        pltpu.make_async_copy(panel_ref.at[pl.ds(0, 64), :], pa_ref.at[y, x], own_sem.at[2]),
+        pltpu.make_async_copy(panel_ref.at[pl.ds(64, 64), :], pb_ref.at[y, x], own_sem.at[3]),
+    ]
+    own_diag = pltpu.make_async_copy(diag_ref, d_ref.at[core, z % 4, z // 4], own_sem.at[1])
+    own_lead = pltpu.make_async_copy(panel_ref.at[pl.ds(0, 8), :], q_ref.at[core, z], own_sem.at[4])
+    mine = z % 4 == y
+    for copy in own:
+        copy.start()
+
+    @pl.when(mine)
     def _():
-        greet((pcol, core))
-
-    lax.fori_loop(1, 16, greet_z, 0)
-    extra = jnp.where(source, 16, 0) - jnp.where(self_lead, 1, 0)
-    pl.semaphore_wait(barrier, 22 + extra)
-
-    def d1(d):
-        return remote(diag_ref, d_ref.at[core, z], d1_send.at[d], d1_recv.at[d], along_z(d))
-
-    def start_d1(d, carry):
-        d1(d).start()
-        return carry
-
-    lax.fori_loop(1, 16, start_d1, 0)
-
-    def q1(t):
-        rows = panel_ref.at[pl.ds(pl.multiple_of(t * 8, 8), 8), :]
-        return remote(rows, q_ref.at[pcol, t], q1_send.at[t], q1_recv.at[0], (t * 2 + pcol, prow))
-
-    own_lead = pltpu.make_async_copy(panel_ref.at[pl.ds(0, 8), :], q_ref.at[core, z], own_sem.at[2])
-
-    @pl.when(source)
-    def _():
-        def start_q1(t, carry):
-            @pl.when(jnp.logical_not(jnp.logical_and(self_lead, t == 0)))
-            def _():
-                q1(t).start()
-            return carry
-
-        lax.fori_loop(0, 16, start_q1, 0)
+        own_diag.start()
+        own_diag.wait()
 
     @pl.when(self_lead)
     def _():
         own_lead.start()
 
-    top, low = panel_ref.at[pl.ds(0, 64), :], panel_ref.at[pl.ds(64, 64), :]
+    for copy in own:
+        copy.wait()
+    extra = jnp.where(source, 16, 0) - jnp.where(self_lead, 1, 0)
+    pl.semaphore_wait(barrier, 22 + extra)
+
+    def q1(d):
+        t = lax.rem(z + d, 16)
+        rows = own_ref.at[pl.ds(pl.multiple_of(t * 8, 8), 8), :]
+        return remote(rows, q_ref.at[pcol, t], q1_send.at[d], q1_recv.at[0], (t * 2 + pcol, prow))
+
+    def each_lead(act):
+        @pl.when(source)
+        def _():
+            each_along_z(lambda d: act(q1(d)))
+
+            @pl.when(jnp.logical_not(self_lead))
+            def _():
+                act(q1(0))
+
+    each_lead(lambda copy: copy.start())
+
+    def d1(d):
+        rows = d_ref.at[core, z % 4, z // 4]
+        return remote(rows, rows, d1_send.at[d], d1_recv.at[d], along_z(d))
+
+    def each_d1(act):
+        @pl.when(mine)
+        def _():
+            each_along_z(lambda d: act(d1(d)))
+
+    each_d1(lambda copy: copy.start())
 
     def xa(d):
-        return remote(top, pa_ref.at[y, x], xa_send.at[d], xa_recv.at[d], along_x(d))
+        return remote(pa_ref.at[y, x], pa_ref.at[y, x], xa_send.at[d], xa_recv.at[d], along_x(d))
 
     def yb(d):
-        return remote(low, pb_ref.at[y, x], yb_send.at[d], yb_recv.at[d], along_y(d))
-
-    own_top = pltpu.make_async_copy(top, pa_ref.at[y, x], own_sem.at[0])
-    own_low = pltpu.make_async_copy(low, pb_ref.at[y, x], own_sem.at[1])
-    for d in (1, 3, 2):
+        return remote(pb_ref.at[y, x], pb_ref.at[y, x], yb_send.at[d], yb_recv.at[d], along_y(d))
+
+    for d in (2, 1, 3):
         xa(d).start()
         yb(d).start()
-    own_top.start()
-    own_low.start()
-    d_ref[core, z] = diag_ref[...]
-
-    def wait_d1(d, carry):
-        d1(d).wait()
-        return carry
-
-    lax.fori_loop(1, 16, wait_d1, 0)
-    d2 = remote(d_ref.at[core], d_ref.at[core], d2_send.at[0], d2_recv.at[0], peer)
-    d2.start()
-
+
+    for d in (1, 3, 2):
+        xa(d).wait_recv()
+        yb(d).wait_recv()
+
+    def ya(d):
+        return remote(pa_ref.at[y], pa_ref.at[y], ya_send.at[d], ya_recv.at[d], along_y(d))
+
+    def xb(d):
+        return remote(pb_ref.at[:, x], pb_ref.at[:, x], xb_send.at[d], xb_recv.at[d], along_x(d))
+
+    for a in range(4):
+        away = lax.rem(z - (4 * a + y) + 16, 16)
+
+        @pl.when(away != 0)
+        def _():
+            d1(away).wait_recv()
+
+    def dy(d):
+        return remote(d_ref.at[core, y], d_ref.at[core, y], dy_send.at[d], dy_recv.at[d], along_y(d))
+
+    for d in (2, 1, 3):
+        dy(d).start()
     @pl.when(jnp.logical_not(self_lead))
     def _():
         remote(q_ref.at[core, z], q_ref.at[core, z], q1_send.at[0], q1_recv.at[0], peer).wait_recv()
@@ -242,56 +293,39 @@
     def q2(d):
         return remote(q_ref.at[core, z], q_ref.at[core, z], q2_send.at[d], q2_recv.at[d], along_z(d))
 
-    def start_q2(d, carry):
-        q2(d).start()
-        return carry
-
-    lax.fori_loop(1, 16, start_q2, 0)
-
-    own_top.wait()
-    own_low.wait()
-    for d in (1, 3, 2):
-        xa(d).wait()
-        yb(d).wait()
-
-    def ya(d):
-        return remote(pa_ref.at[y], pa_ref.at[y], ya_send.at[d], ya_recv.at[d], along_y(d))
-
-    def xb(d):
-        return remote(pb_ref.at[:, x], pb_ref.at[:, x], xb_send.at[d], xb_recv.at[d], along_x(d))
-
-    for d in (1, 3, 2):
+    each_along_z(lambda d: q2(d).start())
+
+    for d in (2, 1, 3):
         ya(d).start()
         xb(d).start()
-
-    d2.wait()
+    for d in (1, 3, 2):
+        dy(d).wait_recv()
+    d2 = remote(d_ref.at[core], d_ref.at[core], d2_send.at[0], d2_recv.at[0], peer)
+    d2.start()
+
+    d2.wait_recv()
     for t in range(16):
         for c in range(2):
-            a_ref[t * 16 + c * 8:t * 16 + c * 8 + 8, :] = d_ref[c, t]
+            a_ref[t * 16 + c * 8:t * 16 + c * 8 + 8, :] = d_ref[c, t % 4, t // 4]
 
     chol_inverse(a_ref, w_ref, e1, r1, u1, y1, e2, r2, u2, y2)
 
-    def wait_q2(d, carry):
-        q2(d).wait()
-        return carry
-
-    lax.fori_loop(1, 16, wait_q2, 0)
+    each_along_z(lambda d: q2(d).wait_recv())
     q3 = remote(q_ref.at[core], q_ref.at[core], q3_send.at[0], q3_recv.at[0], peer)
     q3.start()
-
-    @pl.when(source)
-    def _():
-        def wait_q1(t, carry):
-            @pl.when(jnp.logical_not(jnp.logical_and(self_lead, t == 0)))
-            def _():
-                q1(t).wait_send()
-            return carry
-
-        lax.fori_loop(0, 16, wait_q1, 0)
-
     for d in (1, 3, 2):
-        ya(d).wait()
-        xb(d).wait()
+        ya(d).wait_recv()
+        xb(d).wait_recv()
+        xa(d).wait_send()
+        yb(d).wait_send()
+        ya(d).wait_send()
+        xb(d).wait_send()
+    each_d1(lambda copy: copy.wait_send())
+    for d in (1, 2, 3):
+        dy(d).wait_send()
+    each_along_z(lambda d: q2(d).wait_send())
+    each_lead(lambda copy: copy.wait_send())
+    d2.wait_send()
     q3.wait()
 
 
@@ -307,21 +341,28 @@
     return one(a[0], b[0]) + (one(a[0], b[1]) + one(a[1], b[0]))
 
 
-def update(pa_ref, pb_ref, t_ref, w_ref, q_ref, own_ref, u_ref, s_ref, wh, wl, qh, ql):
-    @pl.when(pl.program_id(0) == 0)
-    def _():
-        w = halves(w_ref[...])
-        wh[...], wl[...] = w
-        qh[...], ql[...] = halves(dot3(halves(q_ref[...]), w))
-        s_ref[...] = dot3(halves(own_ref[...]), w)
-
-    rows = jnp.concatenate([pa_ref[0], pb_ref[0], pa_ref[1], pb_ref[1]], axis=0)
-    solved = dot3(halves(rows), (wh[...], wl[...]))
-    u_ref[...] = t_ref[...] - dot3(halves(solved), (qh[...], ql[...]))
+def update(pa_ref, pb_ref, t_ref, w_ref, q_ref, own_ref, u_ref, s_ref, u_buf, s_buf, u_sem, s_sem):
+    w = halves(w_ref[...])
+    s_buf[...] = dot3(halves(own_ref[...]), w)
+    s_copy = pltpu.make_async_copy(s_buf, s_ref, s_sem.at[0])
+    s_copy.start()
+    q = halves(dot3(halves(q_ref[...]), w))
+    copies = []
+    for i in range(8):
+        rows = jnp.concatenate([pa_ref[2 * i], pb_ref[2 * i], pa_ref[2 * i + 1], pb_ref[2 * i + 1]], axis=0)
+        solved = dot3(halves(rows), w)
+        part = pl.ds(256 * i, 256)
+        u_buf[part, :] = t_ref[part, :] - dot3(halves(solved), q)
+        copy = pltpu.make_async_copy(u_buf.at[part, :], u_ref.at[part, :], u_sem.at[i])
+        copy.start()
+        copies.append(copy)
+    for copy in copies:
+        copy.wait()
+    s_copy.wait()
 
 
 def per_device(diag_block, panel, trailing):
-    hbm = pl.BlockSpec(memory_space=pl.ANY)
+    hbm = pl.BlockSpec(memory_space=pltpu.HBM)
     vmem = pl.BlockSpec(memory_space=pltpu.VMEM)
     dma = pltpu.SemaphoreType.DMA
     pa, pb, q, w = pl.pallas_call(
@@ -332,31 +373,22 @@
             jax.ShapeDtypeStruct((2, 16, 8, 256), F32),
             jax.ShapeDtypeStruct((256, 256), F32),
         ),
-        in_specs=[vmem, hbm],
-        out_specs=(hbm, hbm, hbm, vmem),
-        scratch_shapes=[pltpu.VMEM((2, 16, 8, 256), F32), pltpu.VMEM((256, 256), F32)] + SCRATCH + [
-            dma((16,)), dma((16,)), dma((1,)), dma((1,)), dma((16,)), dma((1,)), dma((16,)), dma((16,)), dma((1,)), dma((1,)),
-            dma((4,)), dma((4,)), dma((4,)), dma((4,)), dma((4,)), dma((4,)), dma((4,)), dma((4,)), dma((3,)),
+        in_specs=[hbm, hbm],
+        out_specs=(vmem,) * 4,
+        scratch_shapes=[pltpu.VMEM((128, 256), F32), pltpu.VMEM((2, 4, 4, 8, 256), F32), pltpu.VMEM((256, 256), F32)] + SCRATCH + [
+            dma((16,)), dma((16,)), dma((4,)), dma((4,)), dma((1,)), dma((1,)), dma((16,)), dma((1,)), dma((16,)), dma((16,)), dma((1,)), dma((1,)),
+            dma((4,)), dma((4,)), dma((4,)), dma((4,)), dma((4,)), dma((4,)), dma((4,)), dma((4,)), dma((5,)),
         ],
+        cost_estimate=pl.CostEstimate(flops=10**10, bytes_accessed=80 * 10**6, transcendentals=0),
         compiler_params=pltpu.CompilerParams(collective_id=0, has_side_effects=True, vmem_limit_bytes=32 << 20),
     )(diag_block, panel)
     pa, pb, q = pa.reshape(16, 64, 256), pb.reshape(16, 64, 256), q.reshape(256, 256)
-
-    def whole(rows):
-        return pl.BlockSpec((rows, 256), lambda i: (0, 0))
-
     return pl.pallas_call(
         update,
-        grid=(8,),
         out_shape=(jax.ShapeDtypeStruct((2048, 256), F32), jax.ShapeDtypeStruct((128, 256), F32)),
-        in_specs=[
-            pl.BlockSpec((2, 64, 256), lambda i: (i, 0, 0)),
-            pl.BlockSpec((2, 64, 256), lambda i: (i, 0, 0)),
-            pl.BlockSpec((256, 256), lambda i: (i, 0)),
-            whole(256), whole(256), whole(128),
-        ],
-        out_specs=(pl.BlockSpec((256, 256), lambda i: (i, 0)), whole(128)),
-        scratch_shapes=[pltpu.VMEM((256, 256), BF16)] * 4,
+        in_specs=[vmem] * 6,
+        out_specs=(hbm, hbm),
+        scratch_shapes=[pltpu.VMEM((2048, 256), F32), pltpu.VMEM((128, 256), F32), dma((8,)), dma((1,))],
         compiler_params=pltpu.CompilerParams(vmem_limit_bytes=32 << 20),
     )(pa, pb, trailing, w, q, panel)
 

time: 55.8 us -> 47.5 us (0.85)
  the two profiles are of different devices: /device:TPU:13 before, /device:TPU:1 now
where the time goes in v2:
time: 47.5 us; the launch traced here: 47.4 us
  Pallas kernels  45 us (95%)
  local copies, waits for them, and re-layouts  1.75 us (4%)
  between operations  0.66 us (1%)
    pallas_call x1, Pallas kernels, per_device(): pl.pallas_call(gather_and_factor, out_shape=(jax.ShapeDtypeStruct((4, 4,...  41.8 us
    pallas_call x1, Pallas kernels, per_device(): pl.pallas_call(update, out_shape=(jax.ShapeDtypeStruct((2048, 256), F32),...  3.14 us
    unnamed x6, local copies, waits for them, and re-layouts  1.75 us

profile of v2, /device:TPU:1, one launch (start us, length us, event | category | flops | bytes accessed | tf_op | source)
XLA Modules:
  0.0 47.4 jit_solution(17762394660879431554)
XLA Ops:
  0.6 0.0 copy-start
  0.6 0.0 copy-start.1
  0.6 1.0 %copy-done.1 = f32[128,256]{1,0:T(8,128)S(1)} copy-done((f32[128,256]{1,0:T(8,128)S(1)}, f32[128,256]{1,0:T(8,128)}, u32[]{:S(2)}) %copy-start.1) | copy-done | bytes 131096
  1.7 0.0 copy-start.2
  1.7 0.7 %copy-done.2 = f32[8,256]{1,0:T(8,128)S(1)} copy-done((f32[8,256]{1,0:T(8,128)S(1)}, f32[8,256]{1,0:T(8,128)}, u32[]{:S(2)}) %copy-start.2) | copy-done | bytes 8216
  2.4 41.8 %shard_map.50 = (f32[4,4,64,256]{3,2,1,0:T(8,128)S(1)}, f32[4,4,64,256]{3,2,1,0:T(8,128)S(1)}, f32[2,16,8,256]{3,2,1,0:T(8,128)S(1)}, f32[256,256]{1,0:T(8,128)S(1)}) custom-call(f32[8,256]{1,0:T(8,128)S(1)} %copy-done.2, f32[128,256]{1,0:T(8,128)S(1)} %copy-done.1), custom_call_target="tpu_custom_call" | custom-call | flops 10000000000 | bytes 80000000 | tf_op jit(solution)/shard_map/pallas_call | solution.py:368
  44.2 0.0 copy-done
  44.2 3.1 %shard_map.51 = (f32[2048,256]{1,0:T(8,128)}, f32[128,256]{1,0:T(8,128)}) custom-call(f32[16,64,256]{2,1,0:T(8,128)S(1)} %bitcast.3, f32[16,64,256]{2,1,0:T(8,128)S(1)} %bitcast.4, f32[2048,256]{1,0:T(8,128)S(1)} %copy-done, f32[256,256]{1,0:T(8,128)S(1)} %get-tuple-element.8.w_ref, f32[256,256]{1,0:T(8,128)S(1)} %bitcast.5, f32[128,256]{1,0:T(8,128)S(1)} %copy-done.1), custom_call_target="tpu_custom_call" | custom-call | tf_op jit(solution)/shard_map/pallas_call | solution.py:386
Async XLA Ops:
  0.6 43.6 %copy-start = (f32[2048,256]{1,0:T(8,128)S(1)}, f32[2048,256]{1,0:T(8,128)}, u32[]{:S(2)}) copy-start(f32[2048,256]{1,0:T(8,128)} %t_ref.1) | copy-start | bytes 6291460
  0.6 1.1 %copy-start.1 = (f32[128,256]{1,0:T(8,128)S(1)}, f32[128,256]{1,0:T(8,128)}, u32[]{:S(2)}) copy-start(f32[128,256]{1,0:T(8,128)} %own_ref.1) | copy-start | bytes 393220
  1.7 0.7 %copy-start.2 = (f32[8,256]{1,0:T(8,128)S(1)}, f32[8,256]{1,0:T(8,128)}, u32[]{:S(2)}) copy-start(f32[8,256]{1,0:T(8,128)} %diag_ref.1) | copy-start | bytes 24580

commit v3 on v2

--- a/solution.py
+++ b/solution.py
@@ -161,9 +161,9 @@
 
 
 def gather_and_factor(
-    diag_ref, panel_ref, pa_ref, pb_ref, q_ref, w_ref,
-    own_ref, d_ref, a_ref, e1, r1, u1, y1, e2, r2, u2, y2,
-    d1_send, d1_recv, dy_send, dy_recv, d2_send, d2_recv, q1_send, q1_recv, q2_send, q2_recv, q3_send, q3_recv,
+    own_ref, pa_ref, pb_ref, q_ref, w_ref,
+    d_ref, a_ref, e1, r1, u1, y1, e2, r2, u2, y2,
+    d1_send, d1_recv, dy_send, dy_recv, q1_send, q1_recv, q2_send, q2_recv, q3_send, q3_recv, w_send, w_recv,
     xa_send, xa_recv, yb_send, yb_recv, ya_send, ya_recv, xb_send, xb_recv, own_sem,
 ):
     prow, pcol = lax.axis_index("prow"), lax.axis_index("pcol")
@@ -171,7 +171,9 @@
     y, x = pcol // 4, pcol % 4
     peer = (z * 2 + 1 - core, pcol)
     source = jnp.logical_and(prow < 16, pcol < 2)
-    self_lead = jnp.logical_and(source, prow == pcol)
+    self_lead = jnp.logical_and(prow == 1, pcol == 1)
+    mine = z % 4 == y
+    factors, leads = core == 0, core == 1
 
     def along_z(d):
         return (lax.rem(z + d, 16) * 2 + core, pcol)
@@ -187,46 +189,53 @@
     def greet(to):
         pl.semaphore_signal(barrier, inc=1, device_id=to, device_id_type=MESH)
 
-    each_along_z(lambda d: greet(along_z(d)))
-
-    @pl.when(jnp.logical_not(self_lead))
-    def _():
-        greet((pcol, core))
+    @pl.when(leads)
+    def _():
+        each_along_z(lambda d: greet(along_z(d)))
+        greet((pcol, 0))
+
+        @pl.when(jnp.logical_not(self_lead))
+        def _():
+            greet((pcol, 1))
+
+    @pl.when(factors)
+    def _():
+        for a in range(4):
+            @pl.when(4 * a + y != z)
+            def _():
+                greet(((4 * a + y) * 2, pcol))
+                greet(((4 * a + y) * 2 + 1, pcol))
 
     for d in (1, 2, 3):
         greet(along_x(d))
         greet(along_y(d))
     greet(peer)
 
+    top, low, diag = own_ref.at[pl.ds(0, 64), :], own_ref.at[pl.ds(64, 64), :], own_ref.at[pl.ds(128, 8), :]
     own = [
-        pltpu.make_async_copy(panel_ref, own_ref, own_sem.at[0]),
-        pltpu.make_async_copy(panel_ref.at[pl.ds(0, 64), :], pa_ref.at[y, x], own_sem.at[2]),
-        pltpu.make_async_copy(panel_ref.at[pl.ds(64, 64), :], pb_ref.at[y, x], own_sem.at[3]),
+        pltpu.make_async_copy(top, pa_ref.at[y, x], own_sem.at[0]),
+        pltpu.make_async_copy(low, pb_ref.at[y, x], own_sem.at[1]),
     ]
-    own_diag = pltpu.make_async_copy(diag_ref, d_ref.at[core, z % 4, z // 4], own_sem.at[1])
-    own_lead = pltpu.make_async_copy(panel_ref.at[pl.ds(0, 8), :], q_ref.at[core, z], own_sem.at[4])
-    mine = z % 4 == y
+    own_diag = pltpu.make_async_copy(diag, d_ref.at[z % 4, z // 4, 0], own_sem.at[2])
+    own_lead = pltpu.make_async_copy(own_ref.at[pl.ds(0, 8), :], q_ref.at[1, z], own_sem.at[3])
     for copy in own:
         copy.start()
 
-    @pl.when(mine)
+    @pl.when(jnp.logical_and(mine, factors))
     def _():
         own_diag.start()
-        own_diag.wait()
 
     @pl.when(self_lead)
     def _():
         own_lead.start()
 
-    for copy in own:
-        copy.wait()
-    extra = jnp.where(source, 16, 0) - jnp.where(self_lead, 1, 0)
-    pl.semaphore_wait(barrier, 22 + extra)
+    others = jnp.where(mine, 15, 0) + jnp.where(leads, 15, 0) + jnp.where(source, 16, 0) - jnp.where(self_lead, 1, 0)
+    pl.semaphore_wait(barrier, 7 + others)
 
     def q1(d):
         t = lax.rem(z + d, 16)
         rows = own_ref.at[pl.ds(pl.multiple_of(t * 8, 8), 8), :]
-        return remote(rows, q_ref.at[pcol, t], q1_send.at[d], q1_recv.at[0], (t * 2 + pcol, prow))
+        return remote(rows, q_ref.at[pcol, t], q1_send.at[d], q1_recv.at[pcol], (t * 2 + 1, prow))
 
     def each_lead(act):
         @pl.when(source)
@@ -240,79 +249,107 @@
     each_lead(lambda copy: copy.start())
 
     def d1(d):
-        rows = d_ref.at[core, z % 4, z // 4]
-        return remote(rows, rows, d1_send.at[d], d1_recv.at[d], along_z(d))
+        to = (lax.rem(z + d, 16) * 2, pcol)
+        return remote(diag, d_ref.at[z % 4, z // 4, core], d1_send.at[d], d1_recv.at[2 * d + core], to)
 
     def each_d1(act):
         @pl.when(mine)
         def _():
             each_along_z(lambda d: act(d1(d)))
 
+            @pl.when(leads)
+            def _():
+                act(d1(0))
+
     each_d1(lambda copy: copy.start())
 
     def xa(d):
-        return remote(pa_ref.at[y, x], pa_ref.at[y, x], xa_send.at[d], xa_recv.at[d], along_x(d))
+        return remote(top, pa_ref.at[y, x], xa_send.at[d], xa_recv.at[d], along_x(d))
 
     def yb(d):
-        return remote(pb_ref.at[y, x], pb_ref.at[y, x], yb_send.at[d], yb_recv.at[d], along_y(d))
+        return remote(low, pb_ref.at[y, x], yb_send.at[d], yb_recv.at[d], along_y(d))
 
     for d in (2, 1, 3):
         xa(d).start()
         yb(d).start()
 
-    for d in (1, 3, 2):
-        xa(d).wait_recv()
-        yb(d).wait_recv()
-
     def ya(d):
         return remote(pa_ref.at[y], pa_ref.at[y], ya_send.at[d], ya_recv.at[d], along_y(d))
 
     def xb(d):
         return remote(pb_ref.at[:, x], pb_ref.at[:, x], xb_send.at[d], xb_recv.at[d], along_x(d))
 
-    for a in range(4):
-        away = lax.rem(z - (4 * a + y) + 16, 16)
-
-        @pl.when(away != 0)
-        def _():
-            d1(away).wait_recv()
+    def second_step():
+        for copy in own:
+            copy.wait()
+        for d in (1, 3, 2):
+            xa(d).wait_recv()
+            yb(d).wait_recv()
+        for d in (2, 1, 3):
+            ya(d).start()
+            xb(d).start()
 
     def dy(d):
-        return remote(d_ref.at[core, y], d_ref.at[core, y], dy_send.at[d], dy_recv.at[d], along_y(d))
-
-    for d in (2, 1, 3):
-        dy(d).start()
-    @pl.when(jnp.logical_not(self_lead))
-    def _():
-        remote(q_ref.at[core, z], q_ref.at[core, z], q1_send.at[0], q1_recv.at[0], peer).wait_recv()
-
-    @pl.when(self_lead)
-    def _():
-        own_lead.wait()
+        return remote(d_ref.at[y], d_ref.at[y], dy_send.at[d], dy_recv.at[d], along_y(d))
 
     def q2(d):
-        return remote(q_ref.at[core, z], q_ref.at[core, z], q2_send.at[d], q2_recv.at[d], along_z(d))
-
-    each_along_z(lambda d: q2(d).start())
-
-    for d in (2, 1, 3):
-        ya(d).start()
-        xb(d).start()
-    for d in (1, 3, 2):
-        dy(d).wait_recv()
-    d2 = remote(d_ref.at[core], d_ref.at[core], d2_send.at[0], d2_recv.at[0], peer)
-    d2.start()
-
-    d2.wait_recv()
-    for t in range(16):
-        for c in range(2):
-            a_ref[t * 16 + c * 8:t * 16 + c * 8 + 8, :] = d_ref[c, t % 4, t // 4]
-
-    chol_inverse(a_ref, w_ref, e1, r1, u1, y1, e2, r2, u2, y2)
-
-    each_along_z(lambda d: q2(d).wait_recv())
-    q3 = remote(q_ref.at[core], q_ref.at[core], q3_send.at[0], q3_recv.at[0], peer)
-    q3.start()
+        return remote(q_ref.at[:, z], q_ref.at[:, z], q2_send.at[d], q2_recv.at[d], along_z(d))
+
+    w_copy = remote(w_ref, w_ref, w_send.at[0], w_recv.at[0], peer)
+    q_copy = remote(q_ref, q_ref, q3_send.at[0], q3_recv.at[0], peer)
+
+    @pl.when(factors)
+    def _():
+        for a in range(4):
+            away = lax.rem(z - (4 * a + y) + 16, 16)
+            for k in range(2):
+                def arrived():
+                    remote(diag, d_ref.at[y, a, k], d1_send.at[0], d1_recv.at[2 * away + k], peer).wait_recv()
+
+                if k == 0:
+                    pl.when(away != 0)(arrived)
+                else:
+                    arrived()
+
+        @pl.when(mine)
+        def _():
+            own_diag.wait()
+
+        for d in (2, 1, 3):
+            dy(d).start()
+        for d in (1, 3, 2):
+            dy(d).wait_recv()
+        second_step()
+        for t in range(16):
+            for c in range(2):
+                a_ref[t * 16 + c * 8:t * 16 + c * 8 + 8, :] = d_ref[t % 4, t // 4, c]
+        chol_inverse(a_ref, w_ref, e1, r1, u1, y1, e2, r2, u2, y2)
+        w_copy.start()
+        for d in (1, 3, 2):
+            dy(d).wait_send()
+        w_copy.wait_send()
+        q_copy.wait_recv()
+
+    @pl.when(leads)
+    def _():
+        second_step()
+        remote(q_ref.at[0, z], q_ref.at[0, z], q1_send.at[0], q1_recv.at[0], peer).wait_recv()
+
+        @pl.when(jnp.logical_not(self_lead))
+        def _():
+            remote(q_ref.at[1, z], q_ref.at[1, z], q1_send.at[0], q1_recv.at[1], peer).wait_recv()
+
+        @pl.when(self_lead)
+        def _():
+            own_lead.wait()
+
+        each_along_z(lambda d: q2(d).start())
+        each_along_z(lambda d: q2(d).wait_recv())
+        q_copy.start()
+        each_along_z(lambda d: q2(d).wait_send())
+        w_copy.wait_recv()
+        q_copy.wait_send()
+
     for d in (1, 3, 2):
         ya(d).wait_recv()
         xb(d).wait_recv()
@@ -321,12 +358,7 @@
         ya(d).wait_send()
         xb(d).wait_send()
     each_d1(lambda copy: copy.wait_send())
-    for d in (1, 2, 3):
-        dy(d).wait_send()
-    each_along_z(lambda d: q2(d).wait_send())
     each_lead(lambda copy: copy.wait_send())
-    d2.wait_send()
-    q3.wait()
 
 
 def halves(v):
@@ -343,7 +375,7 @@
 
 def update(pa_ref, pb_ref, t_ref, w_ref, q_ref, own_ref, u_ref, s_ref, u_buf, s_buf, u_sem, s_sem):
     w = halves(w_ref[...])
-    s_buf[...] = dot3(halves(own_ref[...]), w)
+    s_buf[...] = dot3(halves(own_ref[0:128, :]), w)
     s_copy = pltpu.make_async_copy(s_buf, s_ref, s_sem.at[0])
     s_copy.start()
     q = halves(dot3(halves(q_ref[...]), w))
@@ -362,6 +394,10 @@
 
 
 def per_device(diag_block, panel, trailing):
+    rows, more = panel.shape[0], diag_block.shape[0]
+    low_panel = lax.pad(panel, jnp.float32(0), ((0, more, 0), (0, 0, 0)))
+    high_diag = lax.pad(diag_block, jnp.float32(0), ((rows, 0, 0), (0, 0, 0)))
+    own = jnp.where(lax.broadcasted_iota(jnp.int32, low_panel.shape, 0) < rows, low_panel, high_diag)
     hbm = pl.BlockSpec(memory_space=pltpu.HBM)
     vmem = pl.BlockSpec(memory_space=pltpu.VMEM)
     dma = pltpu.SemaphoreType.DMA
@@ -373,15 +409,15 @@
             jax.ShapeDtypeStruct((2, 16, 8, 256), F32),
             jax.ShapeDtypeStruct((256, 256), F32),
         ),
-        in_specs=[hbm, hbm],
+        in_specs=[vmem],
         out_specs=(vmem,) * 4,
-        scratch_shapes=[pltpu.VMEM((128, 256), F32), pltpu.VMEM((2, 4, 4, 8, 256), F32), pltpu.VMEM((256, 256), F32)] + SCRATCH + [
-            dma((16,)), dma((16,)), dma((4,)), dma((4,)), dma((1,)), dma((1,)), dma((16,)), dma((1,)), dma((16,)), dma((16,)), dma((1,)), dma((1,)),
-            dma((4,)), dma((4,)), dma((4,)), dma((4,)), dma((4,)), dma((4,)), dma((4,)), dma((4,)), dma((5,)),
+        scratch_shapes=[pltpu.VMEM((4, 4, 2, 8, 256), F32), pltpu.VMEM((256, 256), F32)] + SCRATCH + [
+            dma((16,)), dma((32,)), dma((4,)), dma((4,)), dma((16,)), dma((2,)), dma((16,)), dma((16,)), dma((1,)), dma((1,)), dma((1,)), dma((1,)),
+            dma((4,)), dma((4,)), dma((4,)), dma((4,)), dma((4,)), dma((4,)), dma((4,)), dma((4,)), dma((4,)),
         ],
         cost_estimate=pl.CostEstimate(flops=10**10, bytes_accessed=80 * 10**6, transcendentals=0),
         compiler_params=pltpu.CompilerParams(collective_id=0, has_side_effects=True, vmem_limit_bytes=32 << 20),
-    )(diag_block, panel)
+    )(own)
     pa, pb, q = pa.reshape(16, 64, 256), pb.reshape(16, 64, 256), q.reshape(256, 256)
     return pl.pallas_call(
         update,
@@ -390,7 +426,7 @@
         out_specs=(hbm, hbm),
         scratch_shapes=[pltpu.VMEM((2048, 256), F32), pltpu.VMEM((128, 256), F32), dma((8,)), dma((1,))],
         compiler_params=pltpu.CompilerParams(vmem_limit_bytes=32 << 20),
-    )(pa, pb, trailing, w, q, panel)
+    )(pa, pb, trailing, w, q, own)
 
 
 def solution(mesh):

time: 47.5 us -> 44.6 us (0.939)
  the two profiles are of different devices: /device:TPU:1 before, /device:TPU:2 now
where the time goes in v3:
time: 44.6 us; the launch traced here: 44.5 us
  Pallas kernels  42.8 us (96%)
  other arithmetic  1.01 us (2%)
  between operations  0.67 us (2%)
    pallas_call x1, Pallas kernels, per_device(): pl.pallas_call(gather_and_factor, out_shape=(jax.ShapeDtypeStruct((4, 4,...  39.7 us
    pallas_call x1, Pallas kernels, per_device(): pl.pallas_call(update, out_shape=(jax.ShapeDtypeStruct((2048, 256), F32),...  3.14 us
    select_n x1, other arithmetic, per_device(): jnp.where(lax.broadcasted_iota(jnp.int32, low_panel.shape, 0) < rows, low...  1.01 us

profile of v3, /device:TPU:2, one launch (start us, length us, event | category | flops | bytes accessed | tf_op | source)
XLA Modules:
  0.0 44.5 jit_solution(1157684019855334377)
XLA Ops:
  0.6 1.0 %pad_select_fusion.own_ref = f32[136,256]{1,0:T(8,128)S(1)} fusion(f32[8,256]{1,0:T(8,128)} %param.3, f32[128,256]{1,0:T(8,128)} %param.4, pred[136]{0:T(512)(128)(4,1)S(1)} %iota_compare_fusion), kind=kLoop, calls=%fused_computation | loop fusion | flops 34816 | bytes 278664 | tf_op jit(solution)/shard_map/jit(_where)/select_n | solution.py:400
  1.7 0.0 copy-start
  1.7 39.7 %shard_map.50 = (f32[4,4,64,256]{3,2,1,0:T(8,128)S(1)}, f32[4,4,64,256]{3,2,1,0:T(8,128)S(1)}, f32[2,16,8,256]{3,2,1,0:T(8,128)S(1)}, f32[256,256]{1,0:T(8,128)S(1)}) custom-call(f32[136,256]{1,0:T(8,128)S(1)} %pad_select_fusion.own_ref), custom_call_target="tpu_custom_call" | custom-call | flops 10000000000 | bytes 80000000 | tf_op jit(solution)/shard_map/pallas_call | solution.py:404
  41.3 0.0 copy-done
  41.4 3.1 %shard_map.51 = (f32[2048,256]{1,0:T(8,128)}, f32[128,256]{1,0:T(8,128)}) custom-call(f32[16,64,256]{2,1,0:T(8,128)S(1)} %bitcast.3, f32[16,64,256]{2,1,0:T(8,128)S(1)} %bitcast.4, f32[2048,256]{1,0:T(8,128)S(1)} %copy-done, f32[256,256]{1,0:T(8,128)S(1)} %get-tuple-element.8.w_ref, f32[256,256]{1,0:T(8,128)S(1)} %bitcast.5, ...), custom_call_target="tpu_custom_call" | custom-call | tf_op jit(solution)/shard_map/pallas_call | solution.py:422
  (1 shorter events, 0.0 us)
Async XLA Ops:
  1.7 39.7 %copy-start = (f32[2048,256]{1,0:T(8,128)S(1)}, f32[2048,256]{1,0:T(8,128)}, u32[]{:S(2)}) copy-start(f32[2048,256]{1,0:T(8,128)} %t_ref.1) | copy-start | bytes 6291460

commit v4 on v3

--- a/solution.py
+++ b/solution.py
@@ -23,10 +23,6 @@
 
 def dot_nn(a, b):
     return lax.dot_general(a, b, (((1,), (0,)), ((), ())), precision=HI, preferred_element_type=F32)
-
-def dot_nt(a, b):
-    return lax.dot_general(a, b, (((1,), (1,)), ((), ())), precision=HI, preferred_element_type=F32)
-
 
 def update_tn(u):
     rest = u
@@ -40,7 +36,7 @@
     return lax.dot_general(left, right, (((0,), (0,)), ((), ())), preferred_element_type=F32)
 
 
-def stage(e_ref, r_ref, u_ref, y_ref, tiles, unroll=False):
+def stage(e_ref, r_ref, u_ref, y_ref, tiles):
     iota = lax.broadcasted_iota(jnp.int32, (8, 128), 0)
 
     def body(k, carry):
@@ -69,7 +65,7 @@
             if j < 15:
                 gn, sn = divmod(j + 1, 8)
                 across = sub(b[j][gn], sn)
-                p = sub(b[j + 1][gn], sn) - (across * across) * f
+                p = sub(b[j + 1][gn], sn) - (across * f) * across
             g0 = gm[j][0] * f
             g1 = gm[j][1] * f
             gs.append((g0, g1))
@@ -109,26 +105,25 @@
         return carry
 
     r_ref[...] = e_ref[0:16, :]
-    u_ref[...] = jnp.zeros_like(u_ref)
-    if unroll:
-        for k in range(8):
-            body(k, 0)
-    else:
-        lax.fori_loop(0, 8, body, 0)
-
-
-def chol_inverse(a_ref, w_ref, e1, r1, u1, y1, e2, r2, u2, y2, unroll=False):
+    lax.fori_loop(0, 8, body, 0)
+
+
+def prepare(e1, u1, e2, u2):
     eye = (lax.broadcasted_iota(jnp.int32, (H, H), 0) == lax.broadcasted_iota(jnp.int32, (H, H), 1)).astype(F32)
-    e1[0:H, 0:2 * H] = a_ref[0:H, :]
     e1[0:H, 2 * H:3 * H] = eye
     e1[H:, :] = jnp.zeros_like(e1[H:, :])
-    stage(e1, r1, u1, y1, 2, unroll)
-    u12 = y1[:, 0:H]
-    e2[0:H, 0:H] = a_ref[H:2 * H, H:2 * H] - dot_tn(u12, u12)
+    u1[...] = jnp.zeros_like(u1)
     e2[0:H, H:2 * H] = eye
     e2[H:, :] = jnp.zeros_like(e2[H:, :])
+    u2[...] = jnp.zeros_like(u2)
+
+
+def chol_inverse(w_ref, e1, r1, u1, y1, e2, r2, u2, y2):
+    stage(e1, r1, u1, y1, 2)
+    u12 = y1[:, 0:H]
+    e2[0:H, 0:H] = e2[0:H, 0:H] - dot_tn(u12, u12)
     v = dot_tn(u12, y1[:, H:2 * H])
-    stage(e2, r2, u2, y2, 1, unroll)
+    stage(e2, r2, u2, y2, 1)
     w_ref[0:H, 0:H] = y1[:, H:2 * H]
     w_ref[0:H, H:2 * H] = jnp.zeros((H, H), F32)
     w_ref[H:2 * H, 0:H] = -dot_nn(y2[...], v)
@@ -149,6 +144,10 @@
     )
 
 
+def part(rows, right):
+    return rows.at[..., pl.ds(H, H)] if right else rows
+
+
 def each_along_z(act):
     act(8)
 
@@ -162,7 +161,7 @@
 
 def gather_and_factor(
     own_ref, pa_ref, pb_ref, q_ref, w_ref,
-    d_ref, a_ref, e1, r1, u1, y1, e2, r2, u2, y2,
+    d_ref, e1, r1, u1, y1, e2, r2, u2, y2,
     d1_send, d1_recv, dy_send, dy_recv, q1_send, q1_recv, q2_send, q2_recv, q3_send, q3_recv, w_send, w_recv,
     xa_send, xa_recv, yb_send, yb_recv, ya_send, ya_recv, xb_send, xb_recv, own_sem,
 ):
@@ -229,6 +228,10 @@
     def _():
         own_lead.start()
 
+    @pl.when(factors)
+    def _():
+        prepare(e1, u1, e2, u2)
+
     others = jnp.where(mine, 15, 0) + jnp.where(leads, 15, 0) + jnp.where(source, 16, 0) - jnp.where(self_lead, 1, 0)
     pl.semaphore_wait(barrier, 7 + others)
 
@@ -248,18 +251,19 @@
 
     each_lead(lambda copy: copy.start())
 
-    def d1(d):
+    def d1(d, right):
         to = (lax.rem(z + d, 16) * 2, pcol)
-        return remote(diag, d_ref.at[z % 4, z // 4, core], d1_send.at[d], d1_recv.at[2 * d + core], to)
+        return remote(part(diag, right), part(d_ref.at[z % 4, z // 4, core], right), d1_send.at[d], d1_recv.at[2 * d + core], to)
 
     def each_d1(act):
-        @pl.when(mine)
-        def _():
-            each_along_z(lambda d: act(d1(d)))
-
-            @pl.when(leads)
+        for right in (False, True):
+            @pl.when(jnp.logical_and(mine, (z >= 8) == right))
             def _():
-                act(d1(0))
+                each_along_z(lambda d: act(d1(d, right)))
+
+                @pl.when(leads)
+                def _():
+                    act(d1(0, right))
 
     each_d1(lambda copy: copy.start())
 
@@ -289,8 +293,10 @@
             ya(d).start()
             xb(d).start()
 
-    def dy(d):
-        return remote(d_ref.at[y], d_ref.at[y], dy_send.at[d], dy_recv.at[d], along_y(d))
+    def dy(d, right):
+        rows = part(d_ref.at[y, pl.ds(2, 2)], True) if right else d_ref.at[y, pl.ds(0, 2)]
+        k = 4 * int(right) + d
+        return remote(rows, rows, dy_send.at[k], dy_recv.at[k], along_y(d))
 
     def q2(d):
         return remote(q_ref.at[:, z], q_ref.at[:, z], q2_send.at[d], q2_recv.at[d], along_z(d))
@@ -304,7 +310,8 @@
             away = lax.rem(z - (4 * a + y) + 16, 16)
             for k in range(2):
                 def arrived():
-                    remote(diag, d_ref.at[y, a, k], d1_send.at[0], d1_recv.at[2 * away + k], peer).wait_recv()
+                    rows = part(d_ref.at[y, a, k], a >= 2)
+                    remote(rows, rows, d1_send.at[0], d1_recv.at[2 * away + k], peer).wait_recv()
 
                 if k == 0:
                     pl.when(away != 0)(arrived)
@@ -315,18 +322,23 @@
         def _():
             own_diag.wait()
 
-        for d in (2, 1, 3):
-            dy(d).start()
-        for d in (1, 3, 2):
-            dy(d).wait_recv()
+        for right in (False, True):
+            for d in (2, 1, 3):
+                dy(d, right).start()
+        for right in (False, True):
+            for d in (1, 3, 2):
+                dy(d, right).wait_recv()
         second_step()
-        for t in range(16):
-            for c in range(2):
-                a_ref[t * 16 + c * 8:t * 16 + c * 8 + 8, :] = d_ref[t % 4, t // 4, c]
-        chol_inverse(a_ref, w_ref, e1, r1, u1, y1, e2, r2, u2, y2)
+        for t in range(8):
+            for k in range(2):
+                at = t * 16 + k * 8
+                e1[at:at + 8, 0:2 * H] = d_ref[t % 4, t // 4, k]
+                e2[at:at + 8, 0:H] = d_ref[t % 4, 2 + t // 4, k, :, H:2 * H]
+        chol_inverse(w_ref, e1, r1, u1, y1, e2, r2, u2, y2)
         w_copy.start()
-        for d in (1, 3, 2):
-            dy(d).wait_send()
+        for right in (False, True):
+            for d in (1, 3, 2):
+                dy(d, right).wait_send()
         w_copy.wait_send()
         q_copy.wait_recv()
 
@@ -411,8 +423,8 @@
         ),
         in_specs=[vmem],
         out_specs=(vmem,) * 4,
-        scratch_shapes=[pltpu.VMEM((4, 4, 2, 8, 256), F32), pltpu.VMEM((256, 256), F32)] + SCRATCH + [
-            dma((16,)), dma((32,)), dma((4,)), dma((4,)), dma((16,)), dma((2,)), dma((16,)), dma((16,)), dma((1,)), dma((1,)), dma((1,)), dma((1,)),
+        scratch_shapes=[pltpu.VMEM((4, 4, 2, 8, 256), F32)] + SCRATCH + [
+            dma((16,)), dma((32,)), dma((8,)), dma((8,)), dma((16,)), dma((2,)), dma((16,)), dma((16,)), dma((1,)), dma((1,)), dma((1,)), dma((1,)),
             dma((4,)), dma((4,)), dma((4,)), dma((4,)), dma((4,)), dma((4,)), dma((4,)), dma((4,)), dma((4,)),
         ],
         cost_estimate=pl.CostEstimate(flops=10**10, bytes_accessed=80 * 10**6, transcendentals=0),

time: 44.6 us -> 44.5 us (level)
  no operation moved by 1% of the time
where the time goes in v4:
time: 44.5 us; the launch traced here: 44.3 us
  Pallas kernels  42.7 us (96%)
  other arithmetic  1.01 us (2%)
  between operations  0.67 us (2%)
    pallas_call x1, Pallas kernels, per_device(): pl.pallas_call(gather_and_factor, out_shape=(jax.ShapeDtypeStruct((4, 4,...  39.5 us
    pallas_call x1, Pallas kernels, per_device(): pl.pallas_call(update, out_shape=(jax.ShapeDtypeStruct((2048, 256), F32),...  3.14 us
    select_n x1, other arithmetic, per_device(): jnp.where(lax.broadcasted_iota(jnp.int32, low_panel.shape, 0) < rows, low...  1.01 us

profile of v4, /device:TPU:2, one launch (start us, length us, event | category | flops | bytes accessed | tf_op | source)
XLA Modules:
  0.0 44.3 jit_solution(222199515997437523)
XLA Ops:
  0.6 1.0 %pad_select_fusion.own_ref = f32[136,256]{1,0:T(8,128)S(1)} fusion(f32[8,256]{1,0:T(8,128)} %param.3, f32[128,256]{1,0:T(8,128)} %param.4, pred[136]{0:T(512)(128)(4,1)S(1)} %iota_compare_fusion), kind=kLoop, calls=%fused_computation | loop fusion | flops 34816 | bytes 278664 | tf_op jit(solution)/shard_map/jit(_where)/select_n | solution.py:412
  1.7 0.0 copy-start
  1.7 39.5 %shard_map.50 = (f32[4,4,64,256]{3,2,1,0:T(8,128)S(1)}, f32[4,4,64,256]{3,2,1,0:T(8,128)S(1)}, f32[2,16,8,256]{3,2,1,0:T(8,128)S(1)}, f32[256,256]{1,0:T(8,128)S(1)}) custom-call(f32[136,256]{1,0:T(8,128)S(1)} %pad_select_fusion.own_ref), custom_call_target="tpu_custom_call" | custom-call | flops 10000000000 | bytes 80000000 | tf_op jit(solution)/shard_map/pallas_call | solution.py:416
  41.2 0.0 copy-done
  41.2 3.1 %shard_map.51 = (f32[2048,256]{1,0:T(8,128)}, f32[128,256]{1,0:T(8,128)}) custom-call(f32[16,64,256]{2,1,0:T(8,128)S(1)} %bitcast.3, f32[16,64,256]{2,1,0:T(8,128)S(1)} %bitcast.4, f32[2048,256]{1,0:T(8,128)S(1)} %copy-done, f32[256,256]{1,0:T(8,128)S(1)} %get-tuple-element.8.w_ref, f32[256,256]{1,0:T(8,128)S(1)} %bitcast.5, ...), custom_call_target="tpu_custom_call" | custom-call | tf_op jit(solution)/shard_map/pallas_call | solution.py:434
  (1 shorter events, 0.0 us)
Async XLA Ops:
  1.7 39.5 %copy-start = (f32[2048,256]{1,0:T(8,128)S(1)}, f32[2048,256]{1,0:T(8,128)}, u32[]{:S(2)}) copy-start(f32[2048,256]{1,0:T(8,128)} %t_ref.1) | copy-start | bytes 6291460

commit v5 on v4

--- a/solution.py
+++ b/solution.py
@@ -49,41 +49,39 @@
         gm = [[lane(nxt[8 * g:8 * g + 8, :], j) for g in range(2)] for j in range(16)]
         for g in range(2):
             r[g][0] = rot[g]
-        scale = [None, None]
+        done = [[None] * (tiles + 1) for g in range(2)]
         rows = []
         gs = []
+        p = sub(b[0][0], 0)
         for j in range(16):
             gj, sj = divmod(j, 8)
-            if j == 0:
-                p = sub(b[0][0], 0)
-            f = 1.0 / p
-            rs = lax.rsqrt(p)
+            f = lax.rsqrt(p)
             m = [None, None]
             for g in range(gj, 2):
                 m[g] = b[j][g] * f
-            scale[gj] = rs if sj == 0 else jnp.where(iota >= sj, rs, scale[gj])
             if j < 15:
                 gn, sn = divmod(j + 1, 8)
-                across = sub(b[j][gn], sn)
-                p = sub(b[j + 1][gn], sn) - (across * f) * across
+                across = sub(b[j][gn], sn) * f
+                p = sub(b[j + 1][gn], sn) - across * across
             g0 = gm[j][0] * f
             g1 = gm[j][1] * f
             gs.append((g0, g1))
             for c in range(j + 1, 16):
                 gc, sc = divmod(c, 8)
-                a = sub(b[j][gc], sc)
+                a = sub(m[gc], sc)
                 for g in range(gc, 2):
                     b[c][g] = b[c][g] - m[g] * a
                 gm[c][0] = gm[c][0] - g0 * a
                 gm[c][1] = gm[c][1] - g1 * a
-            row = [sub(r[gj][t], sj) for t in range(tiles + 1)]
+            row = [sub(r[gj][t], sj) * f for t in range(tiles + 1)]
             rows.append(row)
+            for t in range(tiles + 1):
+                done[gj][t] = row[t] if sj == 0 else jnp.where(iota >= sj, row[t], done[gj][t])
             for g in range(gj, 2):
-                mm = jnp.where(iota > sj, m[g], 0.0) if g == gj else m[g]
                 if g == gj and sj == 7:
                     continue
                 for t in range(tiles + 1):
-                    r[g][t] = r[g][t] - mm * row[t]
+                    r[g][t] = r[g][t] - m[g] * row[t]
         base = pl.multiple_of((k + 1) * NBK, NBK)
         for g in range(2):
             for t in range(tiles + 1):
@@ -96,7 +94,7 @@
         here = pl.multiple_of(k * NBK, NBK)
         for g in range(2):
             for t in range(tiles + 1):
-                v = r[g][t] * scale[g]
+                v = done[g][t]
                 if t == 0:
                     v = pltpu.roll(v, lax.rem(NBK * (k + 1), H), 1)
                 else:
@@ -118,14 +116,15 @@
     u2[...] = jnp.zeros_like(u2)
 
 
-def chol_inverse(w_ref, e1, r1, u1, y1, e2, r2, u2, y2):
+def chol_inverse(w_ref, upper_done, e1, r1, u1, y1, e2, r2, u2, y2):
     stage(e1, r1, u1, y1, 2)
+    w_ref[0:H, 0:H] = y1[:, H:2 * H]
+    w_ref[0:H, H:2 * H] = jnp.zeros((H, H), F32)
+    upper_done()
     u12 = y1[:, 0:H]
     e2[0:H, 0:H] = e2[0:H, 0:H] - dot_tn(u12, u12)
     v = dot_tn(u12, y1[:, H:2 * H])
     stage(e2, r2, u2, y2, 1)
-    w_ref[0:H, 0:H] = y1[:, H:2 * H]
-    w_ref[0:H, H:2 * H] = jnp.zeros((H, H), F32)
     w_ref[H:2 * H, 0:H] = -dot_nn(y2[...], v)
     w_ref[H:2 * H, H:2 * H] = y2[...]
 
@@ -301,8 +300,22 @@
     def q2(d):
         return remote(q_ref.at[:, z], q_ref.at[:, z], q2_send.at[d], q2_recv.at[d], along_z(d))
 
-    w_copy = remote(w_ref, w_ref, w_send.at[0], w_recv.at[0], peer)
+    def w_copy(i):
+        rows = w_ref.at[pl.ds(128 * i, 128), :]
+        return remote(rows, rows, w_send.at[i], w_recv.at[i], peer)
+
     q_copy = remote(q_ref, q_ref, q3_send.at[0], q3_recv.at[0], peer)
+
+    def finish():
+        for d in (1, 3, 2):
+            ya(d).wait_recv()
+            xb(d).wait_recv()
+            xa(d).wait_send()
+            yb(d).wait_send()
+            ya(d).wait_send()
+            xb(d).wait_send()
+        each_d1(lambda copy: copy.wait_send())
+        each_lead(lambda copy: copy.wait_send())
 
     @pl.when(factors)
     def _():
@@ -325,22 +338,24 @@
         for right in (False, True):
             for d in (2, 1, 3):
                 dy(d, right).start()
+        second_step()
         for right in (False, True):
             for d in (1, 3, 2):
                 dy(d, right).wait_recv()
-        second_step()
         for t in range(8):
             for k in range(2):
                 at = t * 16 + k * 8
                 e1[at:at + 8, 0:2 * H] = d_ref[t % 4, t // 4, k]
                 e2[at:at + 8, 0:H] = d_ref[t % 4, 2 + t // 4, k, :, H:2 * H]
-        chol_inverse(w_ref, e1, r1, u1, y1, e2, r2, u2, y2)
-        w_copy.start()
+        chol_inverse(w_ref, lambda: w_copy(0).start(), e1, r1, u1, y1, e2, r2, u2, y2)
+        w_copy(1).start()
         for right in (False, True):
             for d in (1, 3, 2):
                 dy(d, right).wait_send()
-        w_copy.wait_send()
+        finish()
         q_copy.wait_recv()
+        for i in range(2):
+            w_copy(i).wait_send()
 
     @pl.when(leads)
     def _():
@@ -359,18 +374,10 @@
         each_along_z(lambda d: q2(d).wait_recv())
         q_copy.start()
         each_along_z(lambda d: q2(d).wait_send())
-        w_copy.wait_recv()
+        finish()
         q_copy.wait_send()
-
-    for d in (1, 3, 2):
-        ya(d).wait_recv()
-        xb(d).wait_recv()
-        xa(d).wait_send()
-        yb(d).wait_send()
-        ya(d).wait_send()
-        xb(d).wait_send()
-    each_d1(lambda copy: copy.wait_send())
-    each_lead(lambda copy: copy.wait_send())
+        for i in range(2):
+            w_copy(i).wait_recv()
 
 
 def halves(v):
@@ -424,7 +431,7 @@
         in_specs=[vmem],
         out_specs=(vmem,) * 4,
         scratch_shapes=[pltpu.VMEM((4, 4, 2, 8, 256), F32)] + SCRATCH + [
-            dma((16,)), dma((32,)), dma((8,)), dma((8,)), dma((16,)), dma((2,)), dma((16,)), dma((16,)), dma((1,)), dma((1,)), dma((1,)), dma((1,)),
+            dma((16,)), dma((32,)), dma((8,)), dma((8,)), dma((16,)), dma((2,)), dma((16,)), dma((16,)), dma((1,)), dma((1,)), dma((2,)), dma((2,)),
             dma((4,)), dma((4,)), dma((4,)), dma((4,)), dma((4,)), dma((4,)), dma((4,)), dma((4,)), dma((4,)),
         ],
         cost_estimate=pl.CostEstimate(flops=10**10, bytes_accessed=80 * 10**6, transcendentals=0),

time: 44.5 us -> 44.5 us (level)
  the two profiles are of different devices: /device:TPU:2 before, /device:TPU:1 now
where the time goes in v5:
time: 44.5 us; the launch traced here: 44.2 us
  Pallas kernels  42.5 us (96%)
  other arithmetic  1.01 us (2%)
  between operations  0.67 us (2%)
    pallas_call x1, Pallas kernels, per_device(): pl.pallas_call(gather_and_factor, out_shape=(jax.ShapeDtypeStruct((4, 4,...  39.3 us
    pallas_call x1, Pallas kernels, per_device(): pl.pallas_call(update, out_shape=(jax.ShapeDtypeStruct((2048, 256), F32),...  3.14 us
    select_n x1, other arithmetic, per_device(): jnp.where(lax.broadcasted_iota(jnp.int32, low_panel.shape, 0) < rows, low...  1.01 us

profile of v5, /device:TPU:1, one launch (start us, length us, event | category | flops | bytes accessed | tf_op | source)
XLA Modules:
  0.0 44.2 jit_solution(5865030575970551160)
XLA Ops:
  0.6 1.0 %pad_select_fusion.own_ref = f32[136,256]{1,0:T(8,128)S(1)} fusion(f32[8,256]{1,0:T(8,128)} %param.3, f32[128,256]{1,0:T(8,128)} %param.4, pred[136]{0:T(512)(128)(4,1)S(1)} %iota_compare_fusion), kind=kLoop, calls=%fused_computation | loop fusion | flops 34816 | bytes 278664 | tf_op jit(solution)/shard_map/jit(_where)/select_n | solution.py:419
  1.7 0.0 copy-start
  1.7 39.3 %shard_map.50 = (f32[4,4,64,256]{3,2,1,0:T(8,128)S(1)}, f32[4,4,64,256]{3,2,1,0:T(8,128)S(1)}, f32[2,16,8,256]{3,2,1,0:T(8,128)S(1)}, f32[256,256]{1,0:T(8,128)S(1)}) custom-call(f32[136,256]{1,0:T(8,128)S(1)} %pad_select_fusion.own_ref), custom_call_target="tpu_custom_call" | custom-call | flops 10000000000 | bytes 80000000 | tf_op jit(solution)/shard_map/pallas_call | solution.py:423
  41.0 0.0 copy-done
  41.0 3.1 %shard_map.51 = (f32[2048,256]{1,0:T(8,128)}, f32[128,256]{1,0:T(8,128)}) custom-call(f32[16,64,256]{2,1,0:T(8,128)S(1)} %bitcast.3, f32[16,64,256]{2,1,0:T(8,128)S(1)} %bitcast.4, f32[2048,256]{1,0:T(8,128)S(1)} %copy-done, f32[256,256]{1,0:T(8,128)S(1)} %get-tuple-element.8.w_ref, f32[256,256]{1,0:T(8,128)S(1)} %bitcast.5, ...), custom_call_target="tpu_custom_call" | custom-call | tf_op jit(solution)/shard_map/pallas_call | solution.py:441
  (1 shorter events, 0.0 us)
Async XLA Ops:
  1.7 39.4 %copy-start = (f32[2048,256]{1,0:T(8,128)S(1)}, f32[2048,256]{1,0:T(8,128)}, u32[]{:S(2)}) copy-start(f32[2048,256]{1,0:T(8,128)} %t_ref.1) | copy-start | bytes 6291460
